TPU v7x, 256 devices: a whole 4x4x8 slice. The times are simulated.
256 devices in a mesh: tile: 16 (over y, x_lo, core), fsdp: 16 (over z, x_hi).
Axes of the slice: x: 4 (x_hi: 2, x_lo: 2; x = x_hi * 2 + x_lo), y: 4, z: 8, core: 2. Of those that a mesh axis runs over, the one named last changes fastest.
Arguments:
- tiles_in: bfloat16 [512, 32, 32, 256], P(('tile', 'fsdp')), may hold values from -6 to 6
- first_weight: bfloat16 [512, 2304], P('fsdp'), may hold values from -0.125 to 0.125
- first_bias: float32 [512], replicated, may hold values from -3 to 3
- second_weight: bfloat16 [512, 4608], P('fsdp'), may hold values from -0.09375 to 0.09375
- second_bias: float32 [512], replicated, may hold values from -3 to 3
- side_links: int32 [512, 4, 3], P(('tile', 'fsdp')), may hold values from 0 to 511, as said below
- corner_links: int32 [512, 4, 3], P(('tile', 'fsdp')), may hold values from 0 to 511, as said below
Outputs:
- pooled: bfloat16 [512, 16, 16, 512], P(('tile', 'fsdp'))
Inputs may be any that keep to these rules, and one draw needn't show every extreme that they name: `side_links`: the tile across side s (0 north, 1 east, 2 south, 3 west) of a tile lies on the device one step in that direction, with wrap, in the grid whose rows are the tile index and whose columns are the fsdp index; a tile id g lies on the device numbered g // 2 with the fsdp index fastest. The second entry is a side 0..3, the third a flag 0 or 1. `corner_links`: the tile at corner c (0 north-west, 1 north-east, 2 south-east, 3 south-west) lies on the diagonal device in that direction, with wrap, in the same grid; the second entry is a corner 0..3, the third is 1 where four or five tiles meet and 0 where three meet.
All inputs are finite; a program needn't handle non-finite values.
Results may differ from a plain program's by a relative error of at most 0.0031.
Values may be sent and summed in bfloat16 or wider, within the bound.
A program may use at most 384 MiB of HBM per device.

v0:
```python
import jax
import jax.numpy as jnp
from jax import lax
from jax.sharding import PartitionSpec as P


def with_halo(x, sides, width):
    for axis, dim in sides:
        devices, length = (lax.axis_size(axis), x.shape[dim])
        up = [(i, (i + 1) % devices) for i in range(devices)]
        down = [(j, i) for i, j in up]
        last = lax.slice_in_dim(x, length - width, length, axis=dim)
        initial = lax.slice_in_dim(x, 0, width, axis=dim)
        before = lax.ppermute(last, axis, up)
        after = lax.ppermute(initial, axis, down)
        x = jnp.concatenate([before, x, after], axis=dim)
    return x


def border_parts(field):
    strips = jnp.stack(
        [field[:, 0, :, :], field[:, :, -1, :], field[:, -1, ::-1, :], field[:, ::-1, 0, :]], axis=1
    )
    corners = jnp.stack(
        [field[:, 0, 0, :], field[:, 0, -1, :], field[:, -1, -1, :], field[:, -1, 0, :]], axis=1
    )
    return (strips, corners)


def assemble(field, side_halo, corner_halo):
    upper_row = jnp.concatenate([corner_halo[:, 0:1], side_halo[:, 0], corner_halo[:, 1:2]], axis=1)
    bottom = jnp.concatenate(
        [corner_halo[:, 3:4], side_halo[:, 2, ::-1], corner_halo[:, 2:3]], axis=1
    )
    middle = jnp.concatenate(
        [side_halo[:, 3, ::-1, None, :], field, side_halo[:, 1, :, None, :]], axis=2
    )
    return jnp.concatenate([upper_row[:, None], middle, bottom[:, None]], axis=1)


def surround(field, side_links, corner_links):
    per_device = field.shape[0]
    edge_len = field.shape[1]
    channels = field.shape[3]
    grid_rows = lax.axis_size("tile")
    grid_cols = lax.axis_size("fsdp")
    my_row = lax.axis_index("tile")
    my_col = lax.axis_index("fsdp")

    def locate(tile_ids, pick_index):
        device_id = tile_ids // per_device
        near_row = (device_id // grid_cols - my_row + 1) % grid_rows
        near_col = (device_id % grid_cols - my_col + 1) % grid_cols
        return ((near_row * 3 + near_col) * per_device + tile_ids % per_device) * 4 + pick_index

    strips, corners = border_parts(field)
    bundle = jnp.concatenate([strips, corners[:, :, None, :]], axis=2).reshape(
        1, 1, per_device * 4, edge_len + 1, channels
    )
    nearby = with_halo(bundle, (("tile", 0), ("fsdp", 1)), 1)
    nearby = nearby.reshape(9 * per_device * 4, edge_len + 1, channels)
    near_strips = nearby[:, :edge_len]
    near_corners = nearby[:, edge_len]
    chosen = jnp.take(near_strips, locate(side_links[..., 0], side_links[..., 1]), axis=0)
    chosen = jnp.where(side_links[..., 2][..., None, None] == 1, chosen, chosen[:, :, ::-1])
    corner_halo = jnp.take(near_corners, locate(corner_links[..., 0], corner_links[..., 1]), axis=0)
    corner_halo = jnp.where(
        corner_links[..., 2][..., None] == 1, corner_halo, jnp.zeros_like(corner_halo)
    )
    return assemble(field, chosen, corner_halo)


def convolve(padded, weight_rows):
    edge_len = padded.shape[1] - 2
    channels = padded.shape[3]
    running = jnp.zeros((padded.shape[0], edge_len, edge_len, weight_rows.shape[0]), jnp.float32)
    for row_step in range(3):
        for col_step in range(3):
            tap_index = 3 * row_step + col_step
            window = padded[:, row_step : row_step + edge_len, col_step : col_step + edge_len, :]
            tap_weight = weight_rows[:, tap_index * channels : (tap_index + 1) * channels]
            running = running + lax.dot_general(
                window, tap_weight, (((3,), (1,)), ((), ())), preferred_element_type=jnp.float32
            )
    return running


def finish(pre_act, bias, width):
    act_full = jax.nn.gelu(pre_act + bias, approximate=False)
    half = act_full.shape[1] // 2
    pooled = act_full.reshape(act_full.shape[0], half, 2, half, 2, width).mean(axis=(2, 4))
    return pooled.astype(jnp.bfloat16)


def shards(
    tiles_in, first_weight, first_bias, second_weight, second_bias, side_links, corner_links
):
    padded_first = surround(tiles_in, side_links, corner_links)
    pre_act = (
        convolve(padded_first, lax.all_gather(first_weight, "fsdp", axis=0, tiled=True))
        + first_bias
    )
    hidden = jax.nn.gelu(pre_act, approximate=False).astype(jnp.bfloat16)
    padded_second = surround(hidden, side_links, corner_links)
    weight_rows = lax.all_gather(second_weight, "fsdp", axis=0, tiled=True)
    return finish(convolve(padded_second, weight_rows), second_bias, weight_rows.shape[0])


def solution(mesh):
    placed = (
        P(("tile", "fsdp"), None, None, None),
        P("fsdp", None),
        P(),
        P("fsdp", None),
        P(),
        P(("tile", "fsdp"), None, None),
        P(("tile", "fsdp"), None, None),
    )
    return jax.shard_map(
        shards,
        mesh=mesh,
        in_specs=placed,
        out_specs=P(("tile", "fsdp"), None, None, None),
        check_vma=False,
    )
```

profile of v0, /device:TPU:2, one launch (start us, length us, event | category | flops | bytes accessed | tf_op | source)
XLA Modules:
  0.0 307.6 jit_solution(3010618845285896638)
XLA Ops:
  11.0 2.3 collective-permute-done.1
  13.3 2.5 collective-permute-done
  15.9 7.1 %collective-permute-start.3 = (bf16[3,1,8,33,256]{4,3,2,1,0:T(8,128)(2,1)S(1)}, bf16[3,1,8,33,256]{4,3,2,1,0:T(8,128)(2,1)S(1)}, u32[]{:S(2)}, u32[]{:S(2)}) collective-permute-start(bf16[3,1,8,33,256]{4,3,2,1,0:T(8,128)(2,1)S(1)} %pad_maximum_fusion.13), channel_id=1, source_target_pairs={{1,0},{2,1},{3,2},{4,3},{5,4},{6,5},{7,6},{8,7},{9,8},{10,9},{11,1... | collective-permute-start | bytes 1216520 | tf_op jit(solution)/shard_map/ppermute | solution.py:15
  24.5 18.5 %collective-permute-done.3 = bf16[3,1,8,33,256]{4,3,2,1,0:T(8,128)(2,1)S(1)} collective-permute-done((bf16[3,1,8,33,256]{4,3,2,1,0:T(8,128)(2,1)S(1)}, bf16[3,1,8,33,256]{4,3,2,1,0:T(8,128)(2,1)S(1)}, u32[]{:S(2)}, u32[]{:S(2)}) %collective-permute-start.3) | collective-permute-done | bytes 405536 | tf_op jit(solution)/shard_map/ppermute | solution.py:15
  45.7 2.6 maximum_maximum_fusion.1
  48.3 60.1 %all-gather.3.cloned.1.call-done = bf16[512,2304]{1,0:T(8,128)(2,1)} async-done(((bf16[32,2304]{1,0:T(8,128)(2,1)}), bf16[512,2304]{1,0:T(8,128)(2,1)}) %all-gather.3.cloned.1.call-update) | async-done | bytes 2359312 | tf_op jit(solution)/shard_map/all_gather | solution.py:100
  108.4 1.8 fusion.40
  111.8 2.8 fusion.44
  114.6 2.7 fusion.46
  117.4 2.8 fusion.34
  120.1 2.7 fusion.36
  122.8 2.7 fusion.49
  125.6 10.2 %convert_reduce_fusion = (u32[2,32,512]{2,1,0:T(8,128)S(1)}, f32[2,32,32,512]{3,2,1,0:T(8,128)}) fusion(f32[512]{0:T(512)S(1)} %copy-done.7, bf16[512,2304]{1,0:T(8,128)(2,1)} %all-gather.3.cloned.1.call-done, bf16[2,33,34,256]{3,2,1,0:T(8,128)(2,1)S(1)} %get-tuple-element.20, f32[2,32,32,512]{3,2,1,0:T(8,128)} %fusion.34, f32[2,32,32,512]{3,2,1,0:T(8,128)} %fusion.36, ...), kind=kOutput, calls=%fused_computation.12 | convolution fusion | flops 552566784 | bytes 39192576 | tf_op jit(solution)/shard_map/dot_general | solution.py:82
  135.7 10.5 %fusion.2 = bf16[2,32,32,512]{3,2,1,0:T(8,128)(2,1)S(1)} fusion(f32[2,32,32,512]{3,2,1,0:T(8,128)} %get-tuple-element.48, u32[2,32,512]{2,1,0:T(8,128)S(1)} %get-tuple-element.47), kind=kLoop, calls=%fused_computation.8 | loop fusion | flops 70254592 | bytes 6422528 | tf_op jit(solution)/shard_map/convert_element_type | solution.py:103
  148.1 5.6 %collective-permute-done.5 = bf16[1,1,8,33,512]{4,3,2,1,0:T(8,128)(2,1)S(1)} collective-permute-done((bf16[1,1,8,33,512]{4,3,2,1,0:T(8,128)(2,1)S(1)}, bf16[1,1,8,33,512]{4,3,2,1,0:T(8,128)(2,1)S(1)}, u32[]{:S(2)}, u32[]{:S(2)}) %collective-permute-start.5) | collective-permute-done | bytes 270368 | tf_op jit(solution)/shard_map/ppermute | solution.py:15
  153.7 3.9 %collective-permute-done.4 = bf16[1,1,8,33,512]{4,3,2,1,0:T(8,128)(2,1)S(1)} collective-permute-done((bf16[1,1,8,33,512]{4,3,2,1,0:T(8,128)(2,1)S(1)}, bf16[1,1,8,33,512]{4,3,2,1,0:T(8,128)(2,1)S(1)}, u32[]{:S(2)}, u32[]{:S(2)}) %collective-permute-start.4) | collective-permute-done | bytes 270368 | tf_op jit(solution)/shard_map/ppermute | solution.py:14
  158.0 1.9 collective-permute-start.7
  161.6 53.1 %collective-permute-done.7 = bf16[3,1,8,33,512]{4,2,3,1,0:T(8,128)(2,1)S(1)} collective-permute-done((bf16[3,1,8,33,512]{4,2,3,1,0:T(8,128)(2,1)S(1)}, bf16[3,1,8,33,512]{4,2,3,1,0:T(8,128)(2,1)S(1)}, u32[]{:S(2)}, u32[]{:S(2)}) %collective-permute-start.7) | collective-permute-done | bytes 811040 | tf_op jit(solution)/shard_map/ppermute | solution.py:15
  218.7 3.9 %copy.202 = bf16[72,32,512]{2,1,0:T(8,128)(2,1)} copy(bf16[72,32,512]{2,0,1:T(8,128)(2,1)} %slice.369) | data formatting | bytes 4718592 | tf_op jit(solution)/shard_map/slice | solution.py:62
  222.6 2.3 gather_fusion.3
  226.1 5.0 %maximum_maximum_fusion = (bf16[2,33,34,512]{3,2,1,0:T(8,128)(2,1)}, bf16[2,33,34,512]{3,2,1,0:T(8,128)(2,1)}) fusion(bf16[2,32,1,512]{3,2,1,0:T(2,128)(2,1)S(1)} %copy.205, bf16[2,32,32,512]{3,2,1,0:T(8,128)(2,1)S(1)} %fusion.2, bf16[2,32,1,512]{3,2,1,0:T(2,128)(2,1)S(1)} %copy.204, bf16[2,1,34,512]{3,2,1,0:T(8,128)(2,1)S(1)} %maximum_bitcast_fusion, ...), kind=kLoop, calls=%fused_computation.45 | loop fusion | flops 18382848 | bytes 6963200 | tf_op jit(solution)/shard_map/concatenate | solution.py:38
  231.2 14.6 %all-gather.5.cloned.1.call-done = bf16[512,4608]{1,0:T(8,128)(2,1)} async-done(((bf16[32,4608]{1,0:T(8,128)(2,1)}), bf16[512,4608]{1,0:T(8,128)(2,1)}) %all-gather.5.cloned.1.call-update) | async-done | bytes 4718608 | tf_op jit(solution)/shard_map/all_gather | solution.py:105
  245.8 4.5 %fusion.23 = f32[2,32,32,512]{3,2,1,0:T(8,128)} fusion(bf16[2,32,1,512]{3,2,1,0:T(2,128)(2,1)S(1)} %copy.205, bf16[2,32,32,512]{3,2,1,0:T(8,128)(2,1)S(1)} %fusion.2, bf16[512,4608]{1,0:T(8,128)(2,1)} %all-gather.5.cloned.1.call-done), kind=kOutput, calls=%fused_computation.53 | convolution fusion | flops 1077936128 | bytes 6881280 | tf_op jit(solution)/shard_map/dot_general | solution.py:82
  250.3 3.4 %fusion.25 = f32[2,32,32,512]{3,2,1,0:T(8,128)} fusion(bf16[2,32,32,512]{3,2,1,0:T(8,128)(2,1)S(1)} %fusion.2, bf16[2,32,1,512]{3,2,1,0:T(2,128)(2,1)S(1)} %copy.204, bf16[512,4608]{1,0:T(8,128)(2,1)S(1)} %copy-done.6), kind=kOutput, calls=%fused_computation.56 | convolution fusion | flops 1077936128 | bytes 6946816 | tf_op jit(solution)/shard_map/dot_general | solution.py:82
  253.6 3.4 %fusion.48 = f32[2,32,32,512]{3,2,1,0:T(8,128)} fusion(bf16[2,32,32,512]{3,2,1,0:T(8,128)(2,1)S(1)} %fusion.2, bf16[512,4608]{1,0:T(8,128)(2,1)S(1)} %copy-done.6), kind=kOutput, calls=%fused_computation.91 | convolution fusion | flops 1073741824 | bytes 6815744 | tf_op jit(solution)/shard_map/dot_general | solution.py:82
  257.0 3.2 %fusion.27 = f32[2,32,32,512]{3,2,1,0:T(8,128)} fusion(bf16[2,33,34,512]{3,2,1,0:T(8,128)(2,1)S(1)} %copy-done.3, bf16[512,4608]{1,0:T(8,128)(2,1)S(1)} %copy-done.6), kind=kOutput, calls=%fused_computation.58 | convolution fusion | flops 1073741824 | bytes 6815744 | tf_op jit(solution)/shard_map/dot_general | solution.py:82
  260.2 3.3 %fusion.29 = f32[2,32,32,512]{3,2,1,0:T(8,128)} fusion(bf16[2,33,34,512]{3,2,1,0:T(8,128)(2,1)S(1)} %copy-done.3, bf16[512,4608]{1,0:T(8,128)(2,1)S(1)} %copy-done.6), kind=kOutput, calls=%fused_computation.60 | convolution fusion | flops 1073741824 | bytes 6815744 | tf_op jit(solution)/shard_map/dot_general | solution.py:82
  265.3 3.2 %fusion.19 = f32[2,32,32,512]{3,2,1,0:T(8,128)} fusion(bf16[2,33,34,512]{3,2,1,0:T(8,128)(2,1)S(1)} %copy-done.2, bf16[512,4608]{1,0:T(8,128)(2,1)S(1)} %copy-done.6), kind=kOutput, calls=%fused_computation.48 | convolution fusion | flops 1073741824 | bytes 6815744 | tf_op jit(solution)/shard_map/dot_general | solution.py:82
  268.5 3.3 %fusion.21 = f32[2,32,32,512]{3,2,1,0:T(8,128)} fusion(bf16[2,33,34,512]{3,2,1,0:T(8,128)(2,1)S(1)} %copy-done.2, bf16[512,4608]{1,0:T(8,128)(2,1)S(1)} %copy-done.6), kind=kOutput, calls=%fused_computation.50 | convolution fusion | flops 1073741824 | bytes 6815744 | tf_op jit(solution)/shard_map/dot_general | solution.py:82
  271.8 16.6 %fusion.4 = f32[2,32,32,512]{3,2,1,0:T(8,128)} fusion(f32[2,32,32,512]{3,2,1,0:T(8,128)} %fusion.19, f32[2,32,32,512]{3,2,1,0:T(8,128)} %fusion.21, f32[2,32,32,512]{3,2,1,0:T(8,128)} %fusion.23, f32[2,32,32,512]{3,2,1,0:T(8,128)S(1)} %copy-done.4, f32[2,32,32,512]{3,2,1,0:T(8,128)} %fusion.25, f32[2,32,32,512]{3,2,1,0:T(8,128)} %fusion.27, ...), kind=kOutput, calls=%fused_computation.10 | convolution fusion | flops 1150287872 | bytes 40372224 | tf_op jit(solution)/shard_map/dot_general | solution.py:82
  288.4 5.8 %reshape.38 = f32[2,16,2,16,2,512]{5,4,3,2,1,0:T(2,128)} reshape(f32[2,32,32,512]{3,2,1,0:T(8,128)} %fusion.4) | data formatting | bytes 8388608 | tf_op jit(solution)/shard_map/reshape | solution.py:91
  294.2 5.4 %reduce_sum.9 = f32[2,16,16,512]{3,2,1,0:T(8,128)S(1)} reduce(f32[2,16,2,16,2,512]{5,4,3,2,1,0:T(2,128)} %reshape.38, f32[]{:T(128)} %constant.233.clone.1), dimensions={2,4}, to_apply=%region_0.1 | reduce | flops 786432 | bytes 5242884 | tf_op jit(solution)/shard_map/reduce_sum | solution.py:91
  (116 shorter events, 21.5 us)
Async XLA Ops:
  6.5 101.9 %all-gather.3.cloned.1.call-start = ((), (), s32[]{:S(2)}) async-start(), calls=%async_computation | async-start | bytes 2506752 | tf_op jit(solution)/shard_map/all_gather | solution.py:100
  7.3 238.5 %all-gather.5.cloned.1.call-start = ((), (), s32[]{:S(2)}) async-start(), calls=%async_computation.1 | async-start | bytes 5013504 | tf_op jit(solution)/shard_map/all_gather | solution.py:105
  10.4 2.9 collective-permute-start.1
  10.5 5.4 %collective-permute-start = (bf16[1,1,8,33,256]{4,3,2,1,0:T(8,128)(2,1)S(1)}, bf16[1,1,8,33,256]{4,3,2,1,0:T(8,128)(2,1)S(1)}, u32[]{:S(2)}, u32[]{:S(2)}) collective-permute-start(bf16[1,1,8,33,256]{4,3,2,1,0:T(8,128)(2,1)S(1)} %pad_maximum_fusion.16), channel_id=1, source_target_pairs={{0,16},{16,32},{32,48},{48,64},{64,80},{80,96},{96,112},{112,128},... | collective-permute-start | bytes 405512 | tf_op jit(solution)/shard_map/ppermute | solution.py:14
  15.9 27.1 %collective-permute-start.3 = (bf16[3,1,8,33,256]{4,3,2,1,0:T(8,128)(2,1)S(1)}, bf16[3,1,8,33,256]{4,3,2,1,0:T(8,128)(2,1)S(1)}, u32[]{:S(2)}, u32[]{:S(2)}) collective-permute-start(bf16[3,1,8,33,256]{4,3,2,1,0:T(8,128)(2,1)S(1)} %pad_maximum_fusion.13), channel_id=1, source_target_pairs={{1,0},{2,1},{3,2},{4,3},{5,4},{6,5},{7,6},{8,7},{9,8},{10,9},{11,1... | collective-permute-start | bytes 1216520 | tf_op jit(solution)/shard_map/ppermute | solution.py:15
  23.0 20.0 %collective-permute-start.2 = (bf16[3,1,8,33,256]{4,3,2,1,0:T(8,128)(2,1)S(1)}, bf16[3,1,8,33,256]{4,3,2,1,0:T(8,128)(2,1)S(1)}, u32[]{:S(2)}, u32[]{:S(2)}) collective-permute-start(bf16[3,1,8,33,256]{4,3,2,1,0:T(8,128)(2,1)S(1)} %pad_maximum_fusion.13), channel_id=1, source_target_pairs={{0,1},{1,2},{2,3},{3,4},{4,5},{5,6},{6,7},{7,8},{8,9},{9,10},{10,1... | collective-permute-start | bytes 1216520 | tf_op jit(solution)/shard_map/ppermute | solution.py:14
  43.1 2.6 copy-start
  108.4 1.9 copy-start.5
  108.4 2.6 copy-start.1
  120.1 5.4 %copy-start.7 = (f32[512]{0:T(512)S(1)}, f32[512]{0:T(512)}, u32[]{:S(2)}) copy-start(f32[512]{0:T(512)} %param.9) | copy-start | bytes 6148
  147.0 6.7 %collective-permute-start.5 = (bf16[1,1,8,33,512]{4,3,2,1,0:T(8,128)(2,1)S(1)}, bf16[1,1,8,33,512]{4,3,2,1,0:T(8,128)(2,1)S(1)}, u32[]{:S(2)}, u32[]{:S(2)}) collective-permute-start(bf16[1,1,8,33,512]{4,3,2,1,0:T(8,128)(2,1)S(1)} %pad_maximum_fusion.14), channel_id=1, source_target_pairs={{16,0},{32,16},{48,32},{64,48},{80,64},{96,80},{112,96},{128,112},... | collective-permute-start | bytes 811016 | tf_op jit(solution)/shard_map/ppermute | solution.py:15
  147.6 10.0 %collective-permute-start.4 = (bf16[1,1,8,33,512]{4,3,2,1,0:T(8,128)(2,1)S(1)}, bf16[1,1,8,33,512]{4,3,2,1,0:T(8,128)(2,1)S(1)}, u32[]{:S(2)}, u32[]{:S(2)}) collective-permute-start(bf16[1,1,8,33,512]{4,3,2,1,0:T(8,128)(2,1)S(1)} %pad_maximum_fusion.14), channel_id=1, source_target_pairs={{0,16},{16,32},{32,48},{48,64},{64,80},{80,96},{96,112},{112,128},... | collective-permute-start | bytes 811016 | tf_op jit(solution)/shard_map/ppermute | solution.py:14
  158.0 56.7 %collective-permute-start.7 = (bf16[3,1,8,33,512]{4,2,3,1,0:T(8,128)(2,1)S(1)}, bf16[3,1,8,33,512]{4,2,3,1,0:T(8,128)(2,1)S(1)}, u32[]{:S(2)}, u32[]{:S(2)}) collective-permute-start(bf16[3,1,8,33,512]{4,2,3,1,0:T(8,128)(2,1)S(1)} %copy.195), channel_id=1, source_target_pairs={{1,0},{2,1},{3,2},{4,3},{5,4},{6,5},{7,6},{8,7},{9,8},{10,9},{11,1... | collective-permute-start | bytes 2433032 | tf_op jit(solution)/shard_map/ppermute | solution.py:15
  159.9 55.1 %collective-permute-start.6 = (bf16[3,1,8,33,512]{4,2,3,1,0:T(8,128)(2,1)S(1)}, bf16[3,1,8,33,512]{4,2,3,1,0:T(8,128)(2,1)S(1)}, u32[]{:S(2)}, u32[]{:S(2)}) collective-permute-start(bf16[3,1,8,33,512]{4,2,3,1,0:T(8,128)(2,1)S(1)} %copy.195), channel_id=1, source_target_pairs={{0,1},{1,2},{2,3},{3,4},{4,5},{5,6},{6,7},{7,8},{8,9},{9,10},{10,1... | collective-permute-start | bytes 2433032 | tf_op jit(solution)/shard_map/ppermute | solution.py:14
  245.8 4.5 %copy-start.6 = (bf16[512,4608]{1,0:T(8,128)(2,1)S(1)}, bf16[512,4608]{1,0:T(8,128)(2,1)}, u32[]{:S(2)}) copy-start(bf16[512,4608]{1,0:T(8,128)(2,1)} %all-gather.5.cloned.1.call-done) | copy-start | bytes 14155780
  253.6 3.4 %copy-start.3 = (bf16[2,33,34,512]{3,2,1,0:T(8,128)(2,1)S(1)}, bf16[2,33,34,512]{3,2,1,0:T(8,128)(2,1)}, u32[]{:S(2)}) copy-start(bf16[2,33,34,512]{3,2,1,0:T(8,128)(2,1)} %get-tuple-element.9) | copy-start | bytes 6893572
  263.5 1.8 copy-start.2
  268.5 3.3 %copy-start.4 = (f32[2,32,32,512]{3,2,1,0:T(8,128)S(1)}, f32[2,32,32,512]{3,2,1,0:T(8,128)}, u32[]{:S(2)}) copy-start(f32[2,32,32,512]{3,2,1,0:T(8,128)} %fusion.48) | copy-start | bytes 12582916
  268.5 3.3 %copy-start.8 = (f32[512]{0:T(512)S(1)}, f32[512]{0:T(512)}, u32[]{:S(2)}) copy-start(f32[512]{0:T(512)} %param.11) | copy-start | bytes 6148
Sparse Core Ops, SparseCore 0:
  9.9 98.4 all-gather.2
  111.0 134.7 all-gather.4
where the time goes:
time: 311 us; the launch traced here: 308 us
  waiting for transfers between devices  161 us (52%)
  matrix products  69.3 us (22%)
  other arithmetic  26.7 us (9%)
  local copies, waits for them, and re-layouts  23.2 us (7%)
  between operations  14.2 us (5%)
  starting transfers between devices  12.8 us (4%)
    ppermute x4, waiting for transfers between devices, with_halo(): after = lax.ppermute(initial, axis, down)  79.5 us
    dot_general x18, matrix products, convolve(): lax.dot_general(window, tap_weight, (((3,), (1,)), ((), ())), preferred_e...  69.3 us
    all_gather x1, waiting for transfers between devices, shards(): lax.all_gather(first_weight, 'fsdp', axis=0, tiled=True)  60.1 us
    all_gather x1, waiting for transfers between devices, shards(): weight_rows = lax.all_gather(second_weight, 'fsdp', axis=0, tiled=True)  14.6 us
    convert_element_type x1, other arithmetic, shards(): hidden = jax.nn.gelu(pre_act, approximate=False).astype(jnp.bfloat16)  10.5 us
    ppermute x4, starting transfers between devices, with_halo(): after = lax.ppermute(initial, axis, down)  9.67 us
    concatenate x2, other arithmetic, assemble(): jnp.concatenate([upper_row[:, None], middle, bottom[:, None]], axis=1)  7.63 us
    ppermute x4, waiting for transfers between devices, with_halo(): before = lax.ppermute(last, axis, up)  6.45 us
  transfers between devices with their start and end apart: 10, of which 8 were waited for; matrix products, arithmetic and copies ran while one was open for 21% of the time, Pallas kernels for 0%

commit v1 on v0

v1 whole, which is shorter than its diff:
```python
import functools

import jax
import jax.numpy as jnp
from jax import lax
from jax.experimental import pallas as pl
from jax.experimental.pallas import tpu as pltpu
from jax.sharding import PartitionSpec as P


MESH = pl.DeviceIdType.MESH
BF = jnp.bfloat16
F32 = jnp.float32
CIN, COUT = 256, 512
CW = 768
NU = 9
SENDS = 24 + 8 * NU
ROW_OF_UNIT = (0, 1, 2, 1, 1, 0, 0, 2, 2)


def mod(v, n):
    return lax.rem(v, n)


def gelu(x):
    return 0.5 * x * (1.0 + lax.erf(x * 0.7071067811865476))


def iota(shape, dim):
    return lax.broadcasted_iota(jnp.int32, shape, dim)


def hot(mask):
    return jnp.where(mask, 1.0, 0.0).astype(BF)


def mm_nt(a, b):
    return lax.dot_general(a, b, (((1,), (1,)), ((), ())), preferred_element_type=F32)


def mm(a, b):
    return jnp.dot(a, b, preferred_element_type=F32)


def kernel(
    tiles, w1, b1, w2, b2, side, corner, out,
    wbuf, xin, x1, x2, acc, strips, sel, csel, req_out, req_in, hs1, hc1, hb1, hs2, hc2, hb2,
    lsem, ssem, zssem, zsem, xsem, ysem, sibsem, rqsem, h1sem, h2sem,
):
    tile = lax.axis_index("tile")
    fs = lax.axis_index("fsdp")
    core = mod(tile, 2)
    xlo = mod(lax.div(tile, 2), 2)
    y = lax.div(tile, 4)
    z = lax.div(fs, 2)
    xhi = mod(fs, 2)
    x = xhi * 2 + xlo
    par = mod(y, 2)
    q = par * 2 + xlo

    def dev(xx, yy, cc, zz):
        return {"tile": (yy * 2 + mod(xx, 2)) * 2 + cc, "fsdp": zz * 2 + lax.div(xx, 2)}

    sib = dev(x, y, 1 - core, z)
    ups = dev(x, mod(y + 1, 4), core, z)
    downs = dev(x, mod(y + 3, 4), core, z)
    xdev = [dev(mod(x + k, 4), y, core, z) for k in (1, 2, 3)]
    zdev = [dev(x, y, core, mod(z + k, 8)) for k in (4, 3, 5, 2, 6, 1, 7)]
    no, so = mod(tile + 15, 16), mod(tile + 1, 16)
    ea, we = mod(fs + 1, 16), mod(fs + 15, 16)
    around = [(no, fs), (tile, ea), (so, fs), (tile, we), (no, we), (no, ea), (so, ea), (so, we)]
    around = [{"tile": a, "fsdp": b} for a, b in around]
    opp = (2, 3, 0, 1, 6, 7, 4, 5)

    barrier = pltpu.get_barrier_semaphore()
    partners = [sib, ups, downs] + xdev + zdev + around
    for p in partners:
        pl.semaphore_signal(barrier, inc=1, device_id=p, device_id_type=MESH)

    mine = pl.multiple_of(core * 16, 16)
    tcopy = pltpu.make_async_copy(tiles, xin, lsem.at[NU])
    lcopies = []
    zq, zr = lax.div(z, 4), mod(z, 4)
    for u in range(NU):
        if u < 3:
            src = w1.at[pl.ds(mine, 16), pl.ds(u * CW, CW)]
        else:
            src = w2.at[pl.ds(mine, 16), pl.ds(ROW_OF_UNIT[u] * 2 * CW + ((u + 1) % 2) * CW, CW)]
        lcopies.append(pltpu.make_async_copy(src, wbuf.at[u, core, xhi, zr, zq], lsem.at[u]))
    tcopy.start()

    def own_each(what):
        for u in range(NU):

            @pl.when(zr == mod(q + u, 4))
            def _():
                what(lcopies[u])

    own_each(lambda c: c.start())

    sends = []

    def copy(src, dst, sem, to, out_sem):
        return pltpu.make_async_remote_copy(
            src_ref=src, dst_ref=dst, send_sem=out_sem, recv_sem=sem, device_id=to, device_id_type=MESH
        )

    def send(src, dst, sem, to):
        c = copy(src, dst, sem, to, ssem.at[len(sends)])
        c.start()
        sends.append(c)

    def recv(dst, sem):
        copy(dst, dst, sem, sib, ssem.at[0]).wait_recv()

    lane = iota((8, 128), 1)
    for d in range(4):
        if d % 2 == 0:
            t = lane >> 5
            pos = lane & 31
        else:
            t = (lane >> 3) & 1
            pos = ((lane & 7) << 2) + ((lane >> 4) & 3)
        p = pos if d < 2 else 31 - pos
        rows = []
        for tt in range(2):
            lt = mod(side[tt, d, 0], 2)
            ls = side[tt, d, 1]
            fl = side[tt, d, 2]
            late = ls >= 2
            turn = jnp.logical_xor(fl != 1, late)
            qq = jnp.where(turn, 31 - p, p)
            straight = ls * 64 + lt * 32 + qq
            across = ls * 64 + lt * 8 + ((qq & 3) << 4) + (qq >> 2)
            rows.append(jnp.where(mod(ls, 2) == 0, straight, across))
        row = jnp.where(t == 0, rows[0], rows[1])
        req_out[d] = jnp.where(lane < 64, row, -1)
    for c in range(4):
        row = jnp.full((8, 128), -1, jnp.int32)
        for tt in range(2):
            lt = mod(corner[tt, c, 0], 2)
            lc = corner[tt, c, 1]
            low = jnp.where(lc >= 2, 128, 0)
            end = jnp.where(jnp.logical_or(lc == 1, lc == 2), 31, 0)
            cell = jnp.where(corner[tt, c, 2] == 1, low + lt * 32 + end, -1)
            row = jnp.where(lane == ((c + 2) % 4) * 16 + tt, cell, row)
        req_out[4 + c] = row

    own_each(lambda c: c.wait())
    pl.semaphore_wait(barrier, len(partners))

    for d in range(8):
        send(req_out.at[d], req_in.at[opp[d]], rqsem.at[opp[d]], around[d])

    u0 = mod(z + 4 - q, 4)

    def z_copies(i, u):
        ref = wbuf.at[u, core, xhi, zr, zq]
        return [copy(ref, ref, zsem.at[u, zq], to, zssem.at[i, k]) for k, to in enumerate(zdev)]

    def z_each(what):
        for i in range(3):
            u = u0 + 4 * i

            @pl.when(u < NU)
            def _():
                for c in z_copies(i, u):
                    what(c)

    def x_stage(u):
        m = mod(q + u, 4)
        for h in range(2):

            @pl.when(z != m + 4 * h)
            def _():
                recv(wbuf.at[u, core, xhi, m, h], zsem.at[u, h])

        ref = wbuf.at[u, core, xhi, m]
        for k in range(3):
            send(ref, ref, xsem.at[u, k], xdev[k])

    def y_stage(u):
        for k in range(3):
            xs = mod(x + 3 - k, 4)
            m = mod(par * 2 + mod(xs, 2) + u, 4)
            recv(wbuf.at[u, core, lax.div(xs, 2), m], xsem.at[u, k])
        for h, to in ((0, ups), (1, downs)):
            for i in range(2):
                ref = wbuf.at[u, core, h, mod(par * 2 + u + i, 4)]
                send(ref, ref, ysem.at[u, h, i], to)

    def s_stage(u):
        for h in range(2):
            for i in range(2):
                recv(wbuf.at[u, core, h, mod((1 - par) * 2 + u + i, 4)], ysem.at[u, h, i])
        ref = wbuf.at[u, core]
        send(ref, ref, sibsem.at[u], sib)

    def ready(u):
        recv(wbuf.at[u, 1 - core], sibsem.at[u])

    def weight(u):
        return jnp.transpose(wbuf[u], (3, 2, 1, 0, 4, 5)).reshape(COUT, CW)

    def send_halos(field, ch, hs, hc, hb, sem):
        base = iota((64, 512), 0)
        col = iota((64, 512), 1)
        want = ((base & 31) << 4) + ((base >> 5) << 3)
        north = mm(hot(col == want), field[1, pl.ds(1, 32)].reshape(512, ch))
        south = mm(hot(col == want + 7), field[4, pl.ds(1, 32)].reshape(512, ch))
        st = strips.at[:, pl.ds(0, ch)]
        st[pl.ds(0, 64)] = north.astype(BF)
        st[pl.ds(64, 64)] = field[pl.ds(1, 4), 32].reshape(64, ch)
        st[pl.ds(128, 64)] = south.astype(BF)
        st[pl.ds(192, 64)] = field[pl.ds(1, 4), 1].reshape(64, ch)
        have = st[...]
        landing = (
            hb.at[0, pl.ds(0, 4)], hb.at[2, pl.ds(0, 4)], hb.at[1, pl.ds(0, 4)], hb.at[3, pl.ds(0, 4)],
            hb.at[0, 4], hb.at[0, 5], hb.at[1, 5], hb.at[1, 4],
        )
        for d in range(4):
            got = lax.dot_general(sel[d], have, (((0,), (0,)), ((), ())), preferred_element_type=F32)
            hs[d] = got[0:64].astype(BF).reshape(4, 16, ch)
            send(hs.at[d], landing[opp[d]], sem.at[opp[d]], around[d])
        got = lax.dot_general(csel[...], have, (((0,), (0,)), ((), ())), preferred_element_type=F32)
        hc[...] = got[0:64].astype(BF).reshape(4, 16, ch)
        for c in range(4):
            send(hc.at[c], landing[opp[4 + c]], sem.at[opp[4 + c]], around[4 + c])
        return landing

    def take_halos(field, ch, hb, sem, landing):
        for d in range(8):
            recv(landing[d], sem.at[d])
        field[pl.ds(1, 4), 33] = hb[2, 0:4]
        field[pl.ds(1, 4), 0] = hb[3, 0:4]
        r = iota((544, 96), 0)
        c = iota((544, 96), 1)
        jj = r >> 4
        t = (r >> 3) & 1
        inner = (t << 5) + jj - 1
        want = jnp.where(jj == 0, 64 + t, jnp.where(jj == 33, 80 + t, inner))
        rr = iota((544, ch), 0) & 7
        for n, (to, frm, ih, shift) in enumerate(((0, 4, 0, 1), (5, 1, 7, 543))):
            placed = mm(hot(jnp.logical_and(c == want, (r & 7) == ih)), hb[n].reshape(96, ch))
            moved = pltpu.roll(field[frm].reshape(544, ch).astype(F32), shift, 0)
            field[to] = jnp.where(rr == ih, placed, moved).astype(BF).reshape(34, 16, ch)

    z_each(lambda c: c.start())

    tcopy.wait()
    row = iota((512, 512), 0)
    col = iota((512, 512), 1)
    turn_in = hot(col == ((row & 15) << 5) + (row >> 4))
    for il in range(4):
        part = xin[:, :, il].reshape(512, CIN)
        x1[1 + il, pl.ds(1, 32)] = mm(turn_in, part).astype(BF).reshape(32, 16, CIN)

    for d in range(8):
        recv(req_in.at[d], rqsem.at[d])
    own_row = iota((256, 128), 0)
    for d in range(4):
        sel[d] = hot(own_row == req_in[d][0:1])
    asked = jnp.maximum(jnp.maximum(req_in[4], req_in[5]), jnp.maximum(req_in[6], req_in[7]))
    csel[...] = hot(own_row == asked[0:1])

    land1 = send_halos(x1, CIN, hs1, hc1, hb1, h1sem)
    x_stage(0)
    x_stage(1)
    x_stage(2)
    x_stage(3)
    take_halos(x1, CIN, hb1, h1sem, land1)
    x_stage(4)
    y_stage(0)
    x_stage(5)
    y_stage(1)
    x_stage(6)
    y_stage(2)
    x_stage(7)
    x_stage(8)
    y_stage(3)
    s_stage(0)
    ready(0)

    def first(u, lo, hi):
        def body(il, carry):
            lhs = jnp.concatenate(
                [x1[il + u, pl.ds(b, 32)].reshape(512, CIN) for b in range(3)], axis=1
            )
            d = mm_nt(lhs, weight(u))
            if u == 0:
                acc[il] = d
            elif u == 1:
                acc[il] = acc[il] + d
            else:
                x2[1 + il, pl.ds(1, 32)] = gelu(acc[il] + d + b1[...]).astype(BF).reshape(32, 16, COUT)
            return carry

        lax.fori_loop(lo, hi, body, 0)

    first(0, 0, 2)
    s_stage(1)
    y_stage(4)
    first(0, 2, 4)
    ready(1)
    first(1, 0, 2)
    s_stage(2)
    y_stage(5)
    first(1, 2, 4)
    ready(2)
    first(2, 0, 2)
    s_stage(3)
    y_stage(6)
    first(2, 2, 4)
    s_stage(4)
    y_stage(7)
    land2 = send_halos(x2, COUT, hs2, hc2, hb2, h2sem)
    ready(3)

    INNER = pl.ds(16, 480)

    def taps(a, half, il, j0, nj):
        def window(b):
            return x2[il + a, pl.ds(j0 + b, nj)].reshape(nj * 16, COUT)

        if half == 0:
            return jnp.concatenate([window(0), window(1)[:, 0:256]], axis=1)
        return jnp.concatenate([window(1)[:, 256:512], window(2)], axis=1)

    def inner(u):
        a = ROW_OF_UNIT[u]
        half = (u + 1) % 2

        def body(il, carry):
            d = mm_nt(taps(a, half, il, 1, 30), weight(u))
            if u == 3:
                acc[il, INNER] = d
            else:
                acc[il, INNER] = acc[il, INNER] + d
            return carry

        lax.fori_loop(1 if a == 0 else 0, 3 if a == 2 else 4, body, 0)

    inner(3)
    s_stage(5)
    y_stage(8)
    ready(4)
    inner(4)
    s_stage(6)
    ready(5)
    inner(5)
    s_stage(7)
    ready(6)
    inner(6)
    s_stage(8)
    ready(7)
    inner(7)
    ready(8)
    inner(8)

    take_halos(x2, COUT, hb2, h2sem, land2)
    for a, il in ((0, 0), (2, 3)):
        total = acc[il, INNER]
        for u in range(3, NU):
            if ROW_OF_UNIT[u] == a:
                total = total + mm_nt(taps(a, (u + 1) % 2, il, 1, 30), weight(u))
        acc[il, INNER] = total
    ends = None
    for u in range(3, NU):
        a = ROW_OF_UNIT[u]
        half = (u + 1) % 2

        def column(j):
            def window(b):
                return x2[pl.ds(a, 4), j + b].reshape(64, COUT)

            if half == 0:
                return jnp.concatenate([window(0), window(1)[:, 0:256]], axis=1)
            return jnp.concatenate([window(1)[:, 256:512], window(2)], axis=1)

        d = mm_nt(jnp.concatenate([column(0), column(31)], axis=0), weight(u))
        ends = d if ends is None else ends + d
    for il in range(4):
        acc[il, pl.ds(0, 16)] = ends[il * 16 : il * 16 + 16]
        acc[il, pl.ds(496, 16)] = ends[64 + il * 16 : 80 + il * 16]

    row = iota((256, 256), 0)
    col = iota((256, 256), 1)
    turn_out = hot(col == ((row & 15) << 4) + (row >> 4))
    for half in range(2):
        act = gelu(acc[2 * half] + b2[...]) + gelu(acc[2 * half + 1] + b2[...])
        act = act.reshape(16, 2, 16, COUT)
        pooled = ((act[:, 0] + act[:, 1]) * 0.25).reshape(256, COUT).astype(BF)
        out[:, :, half] = mm(turn_out, pooled).astype(BF).reshape(2, 8, 16, COUT)

    for c in sends:
        c.wait_send()
    z_each(lambda c: c.wait_send())


def shards(tiles_in, first_weight, first_bias, second_weight, second_bias, side_links, corner_links):
    dma = pltpu.SemaphoreType.DMA
    anywhere = pl.BlockSpec(memory_space=pl.ANY)
    vmem = pl.BlockSpec(memory_space=pltpu.VMEM)
    smem = pl.BlockSpec(memory_space=pltpu.SMEM)
    out = pl.pallas_call(
        kernel,
        out_shape=jax.ShapeDtypeStruct((2, 8, 2, 16, COUT), BF),
        in_specs=[anywhere, anywhere, vmem, anywhere, vmem, smem, smem],
        out_specs=vmem,
        scratch_shapes=[
            pltpu.VMEM((NU, 2, 2, 4, 2, 16, CW), BF),
            pltpu.VMEM((2, 8, 4, 32, CIN), BF),
            pltpu.VMEM((6, 34, 16, CIN), BF),
            pltpu.VMEM((6, 34, 16, COUT), BF),
            pltpu.VMEM((4, 512, COUT), F32),
            pltpu.VMEM((256, COUT), BF),
            pltpu.VMEM((4, 256, 128), BF),
            pltpu.VMEM((256, 128), BF),
            pltpu.VMEM((8, 8, 128), jnp.int32),
            pltpu.VMEM((8, 8, 128), jnp.int32),
            pltpu.VMEM((4, 4, 16, CIN), BF),
            pltpu.VMEM((4, 16, CIN), BF),
            pltpu.VMEM((4, 6, 16, CIN), BF),
            pltpu.VMEM((4, 4, 16, COUT), BF),
            pltpu.VMEM((4, 16, COUT), BF),
            pltpu.VMEM((4, 6, 16, COUT), BF),
            dma((NU + 1,)),
            dma((SENDS,)),
            dma((3, 7)),
            dma((NU, 2)),
            dma((NU, 3)),
            dma((NU, 2, 2)),
            dma((NU,)),
            dma((8,)),
            dma((8,)),
            dma((8,)),
        ],
        compiler_params=pltpu.CompilerParams(
            collective_id=0, has_side_effects=True, vmem_limit_bytes=56 * 2**20
        ),
        name="level",
    )(
        tiles_in.reshape(2, 8, 4, 32, CIN),
        first_weight,
        first_bias.reshape(1, COUT),
        second_weight,
        second_bias.reshape(1, COUT),
        side_links,
        corner_links,
    )
    return out.reshape(2, 16, 16, COUT)


def solution(mesh):
    placed = (
        P(("tile", "fsdp"), None, None, None),
        P("fsdp", None),
        P(),
        P("fsdp", None),
        P(),
        P(("tile", "fsdp"), None, None),
        P(("tile", "fsdp"), None, None),
    )
    return jax.shard_map(
        shards,
        mesh=mesh,
        in_specs=placed,
        out_specs=P(("tile", "fsdp"), None, None, None),
        check_vma=False,
    )
```

time: 311 us -> 65.4 us (0.21)
  the two profiles are of different devices: /device:TPU:2 before, /device:TPU:1 now
where the time goes in v1:
time: 65.4 us; the launch traced here: 65.2 us
  Pallas kernels  61.2 us (94%)
  local copies, waits for them, and re-layouts  3.93 us (6%)
    pallas_call x1, Pallas kernels, shards(): pl.pallas_call(kernel, out_shape=jax.ShapeDtypeStruct((2, 8, 2, 16, COUT)...  61.2 us
    unnamed x7, local copies, waits for them, and re-layouts  3.93 us

profile of v1, /device:TPU:1, one launch (start us, length us, event | category | flops | bytes accessed | tf_op | source)
XLA Modules:
  0.0 65.2 jit_solution(7054092455376982169)
XLA Ops:
  0.0 0.0 copy-start
  0.0 0.7 %copy-done = s32[2,4,3]{1,0,2:T(2,128)S(1)} copy-done((s32[2,4,3]{1,0,2:T(2,128)S(1)}, s32[2,4,3]{1,0,2:T(2,128)}, u32[]{:S(2)}) %copy-start) | copy-done | bytes 120
  0.7 0.0 copy-start.1
  0.7 0.7 %copy.8.side = s32[2,4,3]{2,1,0:T(4,128)} copy(s32[2,4,3]{1,0,2:T(2,128)S(1)} %copy-done) | data formatting | bytes 192 | tf_op args[5]
  1.4 0.0 copy-done.1
  1.4 0.7 %copy.9.corner = s32[2,4,3]{2,1,0:T(4,128)} copy(s32[2,4,3]{1,0,2:T(2,128)S(1)} %copy-done.1) | data formatting | bytes 192 | tf_op args[6]
  2.1 61.2 %level.1 = bf16[2,8,2,16,512]{4,3,2,1,0:T(8,128)(2,1)} custom-call(bf16[2,8,4,32,256]{4,3,2,1,0:T(8,128)(2,1)} %bitcast.5, bf16[32,2304]{1,0:T(8,128)(2,1)} %w1.1, f32[1,512]{1,0:T(1,128)} %bitcast.6, bf16[32,4608]{1,0:T(8,128)(2,1)} %w2.1, f32[1,512]{1,0:T(1,128)} %bitcast.7, s32[2,4,3]{2,1,0:T(4,128)} %copy.8.side, s32[2,4,3]{2,1,0:T(4,128)} %copy.9.corner), custom_call_target="tpu_custom_call" | custom-call | tf_op jit(solution)/shard_map/level/pallas_call | solution.py:405
  63.3 1.9 %copy.11 = bf16[2,16,16,512]{3,2,1,0:T(8,128)(2,1)} copy(bf16[2,16,16,512]{3,2,1,0:T(8,128)(2,1)} %bitcast.4) | data formatting | bytes 1048576
Async XLA Ops:
  0.0 0.7 %copy-start = (s32[2,4,3]{1,0,2:T(2,128)S(1)}, s32[2,4,3]{1,0,2:T(2,128)}, u32[]{:S(2)}) copy-start(s32[2,4,3]{1,0,2:T(2,128)} %param.12) | copy-start | bytes 292
  0.7 0.7 %copy-start.1 = (s32[2,4,3]{1,0,2:T(2,128)S(1)}, s32[2,4,3]{1,0,2:T(2,128)}, u32[]{:S(2)}) copy-start(s32[2,4,3]{1,0,2:T(2,128)} %param.13) | copy-start | bytes 292

commit v2 on v1

--- a/solution.py
+++ b/solution.py
@@ -14,7 +14,7 @@
 CIN, COUT = 256, 512
 CW = 768
 NU = 9
-SENDS = 24 + 8 * NU
+SENDS = 24 + 6 * NU
 ROW_OF_UNIT = (0, 1, 2, 1, 1, 0, 0, 2, 2)
 
 
@@ -32,6 +32,10 @@
 
 def hot(mask):
     return jnp.where(mask, 1.0, 0.0).astype(BF)
+
+
+def turned(mask):
+    return jnp.where(mask, 1.0, 0.0).T[0:64].astype(BF)
 
 
 def mm_nt(a, b):
@@ -92,7 +96,7 @@
     def own_each(what):
         for u in range(NU):
 
-            @pl.when(zr == mod(q + u, 4))
+            @pl.when(zr == mod(q + 2 * (u % 2), 4))
             def _():
                 what(lcopies[u])
 
@@ -124,9 +128,9 @@
         p = pos if d < 2 else 31 - pos
         rows = []
         for tt in range(2):
-            lt = mod(side[tt, d, 0], 2)
-            ls = side[tt, d, 1]
-            fl = side[tt, d, 2]
+            lt = mod(side[0, tt, d], 2)
+            ls = side[1, tt, d]
+            fl = side[2, tt, d]
             late = ls >= 2
             turn = jnp.logical_xor(fl != 1, late)
             qq = jnp.where(turn, 31 - p, p)
@@ -138,11 +142,11 @@
     for c in range(4):
         row = jnp.full((8, 128), -1, jnp.int32)
         for tt in range(2):
-            lt = mod(corner[tt, c, 0], 2)
-            lc = corner[tt, c, 1]
+            lt = mod(corner[0, tt, c], 2)
+            lc = corner[1, tt, c]
             low = jnp.where(lc >= 2, 128, 0)
             end = jnp.where(jnp.logical_or(lc == 1, lc == 2), 31, 0)
-            cell = jnp.where(corner[tt, c, 2] == 1, low + lt * 32 + end, -1)
+            cell = jnp.where(corner[2, tt, c] == 1, low + lt * 32 + end, -1)
             row = jnp.where(lane == ((c + 2) % 4) * 16 + tt, cell, row)
         req_out[4 + c] = row
 
@@ -152,23 +156,21 @@
     for d in range(8):
         send(req_out.at[d], req_in.at[opp[d]], rqsem.at[opp[d]], around[d])
 
-    u0 = mod(z + 4 - q, 4)
-
-    def z_copies(i, u):
-        ref = wbuf.at[u, core, xhi, zr, zq]
-        return [copy(ref, ref, zsem.at[u, zq], to, zssem.at[i, k]) for k, to in enumerate(zdev)]
-
-    def z_each(what):
-        for i in range(3):
-            u = u0 + 4 * i
-
-            @pl.when(u < NU)
+    turn = mod(zr + 4 - q, 4)
+    odd = lax.div(turn, 2)
+
+    def z_each(what, groups):
+        for g in groups:
+            u = 2 * g + odd
+
+            @pl.when(jnp.logical_and(mod(turn, 2) == 0, u < NU))
             def _():
-                for c in z_copies(i, u):
-                    what(c)
+                ref = wbuf.at[u, core, xhi, zr, zq]
+                for k, to in enumerate(zdev):
+                    what(copy(ref, ref, zsem.at[u, zq], to, zssem.at[g, k]))
 
     def x_stage(u):
-        m = mod(q + u, 4)
+        m = mod(q + 2 * (u % 2), 4)
         for h in range(2):
 
             @pl.when(z != m + 4 * h)
@@ -182,17 +184,15 @@
     def y_stage(u):
         for k in range(3):
             xs = mod(x + 3 - k, 4)
-            m = mod(par * 2 + mod(xs, 2) + u, 4)
+            m = mod(par * 2 + mod(xs, 2) + 2 * (u % 2), 4)
             recv(wbuf.at[u, core, lax.div(xs, 2), m], xsem.at[u, k])
         for h, to in ((0, ups), (1, downs)):
-            for i in range(2):
-                ref = wbuf.at[u, core, h, mod(par * 2 + u + i, 4)]
-                send(ref, ref, ysem.at[u, h, i], to)
+            ref = wbuf.at[u, core, h, pl.ds(mod(par * 2 + 2 * (u % 2), 4), 2)]
+            send(ref, ref, ysem.at[u, h], to)
 
     def s_stage(u):
         for h in range(2):
-            for i in range(2):
-                recv(wbuf.at[u, core, h, mod((1 - par) * 2 + u + i, 4)], ysem.at[u, h, i])
+            recv(wbuf.at[u, core, h, pl.ds(mod((1 - par) * 2 + 2 * (u % 2), 4), 2)], ysem.at[u, h])
         ref = wbuf.at[u, core]
         send(ref, ref, sibsem.at[u], sib)
 
@@ -219,11 +219,11 @@
             hb.at[0, 4], hb.at[0, 5], hb.at[1, 5], hb.at[1, 4],
         )
         for d in range(4):
-            got = lax.dot_general(sel[d], have, (((0,), (0,)), ((), ())), preferred_element_type=F32)
-            hs[d] = got[0:64].astype(BF).reshape(4, 16, ch)
+            got = mm(sel[d], have)
+            hs[d] = got.astype(BF).reshape(4, 16, ch)
             send(hs.at[d], landing[opp[d]], sem.at[opp[d]], around[d])
-        got = lax.dot_general(csel[...], have, (((0,), (0,)), ((), ())), preferred_element_type=F32)
-        hc[...] = got[0:64].astype(BF).reshape(4, 16, ch)
+        got = mm(csel[...], have)
+        hc[...] = got.astype(BF).reshape(4, 16, ch)
         for c in range(4):
             send(hc.at[c], landing[opp[4 + c]], sem.at[opp[4 + c]], around[4 + c])
         return landing
@@ -245,40 +245,46 @@
             moved = pltpu.roll(field[frm].reshape(544, ch).astype(F32), shift, 0)
             field[to] = jnp.where(rr == ih, placed, moved).astype(BF).reshape(34, 16, ch)
 
-    z_each(lambda c: c.start())
-
-    tcopy.wait()
+
     row = iota((512, 512), 0)
     col = iota((512, 512), 1)
     turn_in = hot(col == ((row & 15) << 5) + (row >> 4))
+    z_each(lambda c: c.start(), (0,))
+    tcopy.wait()
     for il in range(4):
         part = xin[:, :, il].reshape(512, CIN)
         x1[1 + il, pl.ds(1, 32)] = mm(turn_in, part).astype(BF).reshape(32, 16, CIN)
+    z_each(lambda c: c.start(), (1,))
 
     for d in range(8):
         recv(req_in.at[d], rqsem.at[d])
     own_row = iota((256, 128), 0)
     for d in range(4):
-        sel[d] = hot(own_row == req_in[d][0:1])
+        sel[d] = turned(own_row == req_in[d][0:1])
     asked = jnp.maximum(jnp.maximum(req_in[4], req_in[5]), jnp.maximum(req_in[6], req_in[7]))
-    csel[...] = hot(own_row == asked[0:1])
-
+    csel[...] = turned(own_row == asked[0:1])
     land1 = send_halos(x1, CIN, hs1, hc1, hb1, h1sem)
-    x_stage(0)
-    x_stage(1)
-    x_stage(2)
-    x_stage(3)
+
+    def pass_on(k):
+        if 0 <= k < NU:
+            x_stage(k)
+        if 0 <= k - 3 < NU:
+            y_stage(k - 3)
+        if 0 <= k - 6 < NU:
+            s_stage(k - 6)
+
+    pass_on(0)
+    z_each(lambda c: c.start(), (2,))
+    pass_on(1)
+    z_each(lambda c: c.start(), (3,))
+    pass_on(2)
+    z_each(lambda c: c.start(), (4,))
     take_halos(x1, CIN, hb1, h1sem, land1)
-    x_stage(4)
-    y_stage(0)
-    x_stage(5)
-    y_stage(1)
-    x_stage(6)
-    y_stage(2)
-    x_stage(7)
-    x_stage(8)
-    y_stage(3)
-    s_stage(0)
+    pass_on(3)
+    pass_on(4)
+    pass_on(5)
+    pass_on(6)
+    pass_on(7)
     ready(0)
 
     def first(u, lo, hi):
@@ -297,22 +303,11 @@
 
         lax.fori_loop(lo, hi, body, 0)
 
-    first(0, 0, 2)
-    s_stage(1)
-    y_stage(4)
-    first(0, 2, 4)
-    ready(1)
-    first(1, 0, 2)
-    s_stage(2)
-    y_stage(5)
-    first(1, 2, 4)
-    ready(2)
-    first(2, 0, 2)
-    s_stage(3)
-    y_stage(6)
-    first(2, 2, 4)
-    s_stage(4)
-    y_stage(7)
+    for u in range(3):
+        first(u, 0, 4)
+        pass_on(8 + u)
+        if u < 2:
+            ready(u + 1)
     land2 = send_halos(x2, COUT, hs2, hc2, hb2, h2sem)
     ready(3)
 
@@ -326,7 +321,7 @@
             return jnp.concatenate([window(0), window(1)[:, 0:256]], axis=1)
         return jnp.concatenate([window(1)[:, 256:512], window(2)], axis=1)
 
-    def inner(u):
+    def inner(u, lo, hi):
         a = ROW_OF_UNIT[u]
         half = (u + 1) % 2
 
@@ -338,63 +333,70 @@
                 acc[il, INNER] = acc[il, INNER] + d
             return carry
 
-        lax.fori_loop(1 if a == 0 else 0, 3 if a == 2 else 4, body, 0)
-
-    inner(3)
-    s_stage(5)
-    y_stage(8)
+        lax.fori_loop(lo, hi, body, 0)
+
+    def rest(units):
+        ends = None
+        for u in units:
+            a = ROW_OF_UNIT[u]
+            half = (u + 1) % 2
+
+            def column(j):
+                def window(b):
+                    return x2[pl.ds(a, 4), j + b].reshape(64, COUT)
+
+                if half == 0:
+                    return jnp.concatenate([window(0), window(1)[:, 0:256]], axis=1)
+                return jnp.concatenate([window(1)[:, 256:512], window(2)], axis=1)
+
+            d = mm_nt(jnp.concatenate([column(0), column(31)], axis=0), weight(u))
+            ends = d if ends is None else ends + d
+            if a == 0:
+                acc[0, INNER] = acc[0, INNER] + mm_nt(taps(a, half, 0, 1, 30), weight(u))
+        for il in range(4):
+            acc[il, pl.ds(0, 16)] = ends[il * 16 : il * 16 + 16]
+            acc[il, pl.ds(496, 16)] = ends[64 + il * 16 : 80 + il * 16]
+
+    def whole(u, lo, hi):
+        def body(il, carry):
+            acc[il] = acc[il] + mm_nt(taps(ROW_OF_UNIT[u], (u + 1) % 2, il, 0, 32), weight(u))
+            return carry
+
+        lax.fori_loop(lo, hi, body, 0)
+
+    inner(3, 0, 4)
+    pass_on(11)
     ready(4)
-    inner(4)
-    s_stage(6)
+    inner(4, 0, 4)
+    pass_on(12)
     ready(5)
-    inner(5)
-    s_stage(7)
+    inner(5, 1, 4)
+    pass_on(13)
+    take_halos(x2, COUT, hb2, h2sem, land2)
+    rest((3, 4, 5))
     ready(6)
-    inner(6)
-    s_stage(8)
+    whole(6, 0, 4)
+    pass_on(14)
     ready(7)
-    inner(7)
+    whole(7, 0, 4)
     ready(8)
-    inner(8)
-
-    take_halos(x2, COUT, hb2, h2sem, land2)
-    for a, il in ((0, 0), (2, 3)):
-        total = acc[il, INNER]
-        for u in range(3, NU):
-            if ROW_OF_UNIT[u] == a:
-                total = total + mm_nt(taps(a, (u + 1) % 2, il, 1, 30), weight(u))
-        acc[il, INNER] = total
-    ends = None
-    for u in range(3, NU):
-        a = ROW_OF_UNIT[u]
-        half = (u + 1) % 2
-
-        def column(j):
-            def window(b):
-                return x2[pl.ds(a, 4), j + b].reshape(64, COUT)
-
-            if half == 0:
-                return jnp.concatenate([window(0), window(1)[:, 0:256]], axis=1)
-            return jnp.concatenate([window(1)[:, 256:512], window(2)], axis=1)
-
-        d = mm_nt(jnp.concatenate([column(0), column(31)], axis=0), weight(u))
-        ends = d if ends is None else ends + d
-    for il in range(4):
-        acc[il, pl.ds(0, 16)] = ends[il * 16 : il * 16 + 16]
-        acc[il, pl.ds(496, 16)] = ends[64 + il * 16 : 80 + il * 16]
 
     row = iota((256, 256), 0)
     col = iota((256, 256), 1)
     turn_out = hot(col == ((row & 15) << 4) + (row >> 4))
     for half in range(2):
-        act = gelu(acc[2 * half] + b2[...]) + gelu(acc[2 * half + 1] + b2[...])
+        act = None
+        for il in (2 * half, 2 * half + 1):
+            last = mm_nt(taps(2, 1, il, 0, 32), weight(8))
+            part = gelu(acc[il] + last + b2[...])
+            act = part if act is None else act + part
         act = act.reshape(16, 2, 16, COUT)
         pooled = ((act[:, 0] + act[:, 1]) * 0.25).reshape(256, COUT).astype(BF)
         out[:, :, half] = mm(turn_out, pooled).astype(BF).reshape(2, 8, 16, COUT)
 
     for c in sends:
         c.wait_send()
-    z_each(lambda c: c.wait_send())
+    z_each(lambda c: c.wait_send(), range(5))
 
 
 def shards(tiles_in, first_weight, first_bias, second_weight, second_bias, side_links, corner_links):
@@ -414,8 +416,8 @@
             pltpu.VMEM((6, 34, 16, COUT), BF),
             pltpu.VMEM((4, 512, COUT), F32),
             pltpu.VMEM((256, COUT), BF),
-            pltpu.VMEM((4, 256, 128), BF),
-            pltpu.VMEM((256, 128), BF),
+            pltpu.VMEM((4, 64, 256), BF),
+            pltpu.VMEM((64, 256), BF),
             pltpu.VMEM((8, 8, 128), jnp.int32),
             pltpu.VMEM((8, 8, 128), jnp.int32),
             pltpu.VMEM((4, 4, 16, CIN), BF),
@@ -426,10 +428,10 @@
             pltpu.VMEM((4, 6, 16, COUT), BF),
             dma((NU + 1,)),
             dma((SENDS,)),
-            dma((3, 7)),
+            dma((5, 7)),
             dma((NU, 2)),
             dma((NU, 3)),
-            dma((NU, 2, 2)),
+            dma((NU, 2)),
             dma((NU,)),
             dma((8,)),
             dma((8,)),
@@ -445,8 +447,8 @@
         first_bias.reshape(1, COUT),
         second_weight,
         second_bias.reshape(1, COUT),
-        side_links,
-        corner_links,
+        jnp.transpose(side_links, (2, 0, 1)),
+        jnp.transpose(corner_links, (2, 0, 1)),
     )
     return out.reshape(2, 16, 16, COUT)
 

time: 65.4 us -> 61.8 us (0.945)
  local copies, waits for them, and re-layouts: 3.93 us -> 1.87 us
  Pallas kernels: 61.2 us -> 59.8 us
    unnamed x7 -> x1, local copies, waits for them, and re-layouts: 3.93 us -> 1.87 us
    pallas_call x1, Pallas kernels: 61.2 us -> 59.8 us  [shards(): pl.pallas_call(kernel, out_shape=jax.ShapeDtypeStruct((2, 8, 2, 16, COUT)...]
where the time goes in v2:
time: 61.8 us; the launch traced here: 61.7 us
  Pallas kernels  59.8 us (97%)
  local copies, waits for them, and re-layouts  1.87 us (3%)
    pallas_call x1, Pallas kernels, shards(): pl.pallas_call(kernel, out_shape=jax.ShapeDtypeStruct((2, 8, 2, 16, COUT)...  59.8 us
    unnamed x1, local copies, waits for them, and re-layouts  1.87 us

profile of v2, /device:TPU:1, one launch (start us, length us, event | category | flops | bytes accessed | tf_op | source)
XLA Modules:
  0.0 61.7 jit_solution(1899389007629234831)
XLA Ops:
  0.0 59.8 %level.1 = bf16[2,8,2,16,512]{4,3,2,1,0:T(8,128)(2,1)} custom-call(bf16[2,8,4,32,256]{4,3,2,1,0:T(8,128)(2,1)} %bitcast.7, bf16[32,2304]{1,0:T(8,128)(2,1)} %w1.1, f32[1,512]{1,0:T(1,128)} %bitcast.10, bf16[32,4608]{1,0:T(8,128)(2,1)} %w2.1, f32[1,512]{1,0:T(1,128)} %bitcast.11, s32[3,2,4]{2,1,0:T(2,128)} %bitcast.8, s32[3,2,4]{2,1,0:T(2,128)} %bitcast.9), custom_call_target="tpu_custom_call" | custom-call | tf_op jit(solution)/shard_map/level/pallas_call | solution.py:407
  59.8 1.9 %copy.9 = bf16[2,16,16,512]{3,2,1,0:T(8,128)(2,1)} copy(bf16[2,16,16,512]{3,2,1,0:T(8,128)(2,1)} %bitcast.6) | data formatting | bytes 1048576

commit v3 on v2

--- a/solution.py
+++ b/solution.py
@@ -268,10 +268,10 @@
     def pass_on(k):
         if 0 <= k < NU:
             x_stage(k)
-        if 0 <= k - 3 < NU:
-            y_stage(k - 3)
-        if 0 <= k - 6 < NU:
-            s_stage(k - 6)
+        if 0 <= k - 2 < NU:
+            y_stage(k - 2)
+        if 0 <= k - 5 < NU:
+            s_stage(k - 5)
 
     pass_on(0)
     z_each(lambda c: c.start(), (2,))
@@ -284,7 +284,6 @@
     pass_on(4)
     pass_on(5)
     pass_on(6)
-    pass_on(7)
     ready(0)
 
     def first(u, lo, hi):
@@ -305,11 +304,10 @@
 
     for u in range(3):
         first(u, 0, 4)
-        pass_on(8 + u)
-        if u < 2:
-            ready(u + 1)
-    land2 = send_halos(x2, COUT, hs2, hc2, hb2, h2sem)
-    ready(3)
+        if u == 2:
+            land2 = send_halos(x2, COUT, hs2, hc2, hb2, h2sem)
+        pass_on(7 + u)
+        ready(u + 1)
 
     INNER = pl.ds(16, 480)
 
@@ -365,18 +363,18 @@
         lax.fori_loop(lo, hi, body, 0)
 
     inner(3, 0, 4)
-    pass_on(11)
+    pass_on(10)
     ready(4)
     inner(4, 0, 4)
-    pass_on(12)
+    pass_on(11)
     ready(5)
     inner(5, 1, 4)
-    pass_on(13)
+    pass_on(12)
     take_halos(x2, COUT, hb2, h2sem, land2)
     rest((3, 4, 5))
     ready(6)
     whole(6, 0, 4)
-    pass_on(14)
+    pass_on(13)
     ready(7)
     whole(7, 0, 4)
     ready(8)

time: 61.8 us -> 61.9 us (level)
  no operation moved by 1% of the time
where the time goes in v3:
time: 61.9 us; the launch traced here: 61.7 us
  Pallas kernels  59.8 us (97%)
  local copies, waits for them, and re-layouts  1.87 us (3%)
    pallas_call x1, Pallas kernels, shards(): pl.pallas_call(kernel, out_shape=jax.ShapeDtypeStruct((2, 8, 2, 16, COUT)...  59.8 us
    unnamed x1, local copies, waits for them, and re-layouts  1.87 us

profile of v3, /device:TPU:1, one launch (start us, length us, event | category | flops | bytes accessed | tf_op | source)
XLA Modules:
  0.0 61.7 jit_solution(6053198041390469181)
XLA Ops:
  0.0 59.8 %level.1 = bf16[2,8,2,16,512]{4,3,2,1,0:T(8,128)(2,1)} custom-call(bf16[2,8,4,32,256]{4,3,2,1,0:T(8,128)(2,1)} %bitcast.7, bf16[32,2304]{1,0:T(8,128)(2,1)} %w1.1, f32[1,512]{1,0:T(1,128)} %bitcast.10, bf16[32,4608]{1,0:T(8,128)(2,1)} %w2.1, f32[1,512]{1,0:T(1,128)} %bitcast.11, s32[3,2,4]{2,1,0:T(2,128)} %bitcast.8, s32[3,2,4]{2,1,0:T(2,128)} %bitcast.9), custom_call_target="tpu_custom_call" | custom-call | tf_op jit(solution)/shard_map/level/pallas_call | solution.py:405
  59.8 1.9 %copy.9 = bf16[2,16,16,512]{3,2,1,0:T(8,128)(2,1)} copy(bf16[2,16,16,512]{3,2,1,0:T(8,128)(2,1)} %bitcast.6) | data formatting | bytes 1048576

commit v4 on v3

--- a/solution.py
+++ b/solution.py
@@ -266,12 +266,12 @@
     land1 = send_halos(x1, CIN, hs1, hc1, hb1, h1sem)
 
     def pass_on(k):
+        if 0 <= k - 5 < NU:
+            s_stage(k - 5)
         if 0 <= k < NU:
             x_stage(k)
         if 0 <= k - 2 < NU:
             y_stage(k - 2)
-        if 0 <= k - 5 < NU:
-            s_stage(k - 5)
 
     pass_on(0)
     z_each(lambda c: c.start(), (2,))

time: 61.9 us -> 61.5 us (level)
  no operation moved by 1% of the time
where the time goes in v4:
time: 61.5 us; the launch traced here: 61.3 us
  Pallas kernels  59.4 us (97%)
  local copies, waits for them, and re-layouts  1.87 us (3%)
    pallas_call x1, Pallas kernels, shards(): pl.pallas_call(kernel, out_shape=jax.ShapeDtypeStruct((2, 8, 2, 16, COUT)...  59.4 us
    unnamed x1, local copies, waits for them, and re-layouts  1.87 us

profile of v4, /device:TPU:1, one launch (start us, length us, event | category | flops | bytes accessed | tf_op | source)
XLA Modules:
  0.0 61.3 jit_solution(13403162710229376855)
XLA Ops:
  0.0 59.4 %level.1 = bf16[2,8,2,16,512]{4,3,2,1,0:T(8,128)(2,1)} custom-call(bf16[2,8,4,32,256]{4,3,2,1,0:T(8,128)(2,1)} %bitcast.7, bf16[32,2304]{1,0:T(8,128)(2,1)} %w1.1, f32[1,512]{1,0:T(1,128)} %bitcast.10, bf16[32,4608]{1,0:T(8,128)(2,1)} %w2.1, f32[1,512]{1,0:T(1,128)} %bitcast.11, s32[3,2,4]{2,1,0:T(2,128)} %bitcast.8, s32[3,2,4]{2,1,0:T(2,128)} %bitcast.9), custom_call_target="tpu_custom_call" | custom-call | tf_op jit(solution)/shard_map/level/pallas_call | solution.py:405
  59.5 1.9 %copy.9 = bf16[2,16,16,512]{3,2,1,0:T(8,128)(2,1)} copy(bf16[2,16,16,512]{3,2,1,0:T(8,128)(2,1)} %bitcast.6) | data formatting | bytes 1048576
